TPU v7x, 32 devices: a whole 2x2x4 slice. The times are simulated.
32 devices in a mesh: groups: 1, expert: 16 (over z, y, x), dp: 2 (over core).
Axes of the slice: x: 2, y: 2, z: 4, core: 2. Of those that a mesh axis runs over, the one named last changes fastest.
Arguments:
- tokens: bfloat16 [2048, 3584], P(('groups', 'expert', 'dp')), may hold values from -6 to 6
- router_logits: float32 [2048, 8], P(('groups', 'expert', 'dp')), may hold values from -6 to 6
- expert_ids: int32 [2048, 8], P(('groups', 'expert', 'dp')), may hold values from 0 to 15, all different within a row; in each aligned block of 64 rows (0 to 63, 64 to 127, ...) at most 40 rows name the same one
- gate_up: bfloat16 [16, 2, 3584, 1024], P('expert', None, None, 'dp'), may hold values from -0.09375 to 0.09375
- down_proj: bfloat16 [16, 1024, 3584], P('expert', 'dp'), may hold values from -0.1875 to 0.1875
- latent_cache: bfloat16 [32, 512, 576], P(('groups', 'expert', 'dp')), may hold values from -4 to 4
- cache_len: int32 [32], P(('groups', 'expert', 'dp')), may hold values from 128 to 510, as said below
- new_latent: bfloat16 [32, 2, 576], P(('groups', 'expert', 'dp')), may hold values from -4 to 4
- queries: bfloat16 [32, 2, 128, 576], P(('groups', 'expert', 'dp')), may hold values from -28 to 28
Outputs:
- mixed_tokens: bfloat16 [2048, 3584], P(('groups', 'expert', 'dp'))
- context: bfloat16 [32, 2, 128, 512], P(('groups', 'expert', 'dp'))
Inputs may be any that keep to these rules, and one draw needn't show every extreme that they name: `expert_ids`: each token names 8 different experts; among the 64 tokens of one device no expert is named by more than 40 tokens, a bound that some block reaches. `cache_len`: some request has exactly 510 live rows and some exactly 128.
All inputs are finite; a program needn't handle non-finite values.
Results may differ from a plain program's by a relative error of at most 0.008.
Values may be sent and summed in bfloat16 or wider, within the bound.
A program may use at most 128 MiB of HBM per device.

v0:
```python
import jax
import jax.numpy as jnp
from jax import lax
from jax.sharding import PartitionSpec as P

LATENT = 512


softmax_scale = 192.0 ** (-0.5)
route_scale = 2.5
excluded = -1e30


def routing_gates(router_logits):
    affinity = jax.nn.sigmoid(router_logits)
    return route_scale * affinity / jnp.sum(affinity, axis=1, keepdims=True)


def hidden_units(row_block, gate_up_half):
    gate_and_up = jnp.einsum(
        "rd,gdf->rgf", row_block, gate_up_half, preferred_element_type=jnp.float32
    )
    return (jax.nn.silu(gate_and_up[:, 0]) * gate_and_up[:, 1]).astype(jnp.bfloat16)


def latent_attention(latent_cache, cache_len, new_latent, queries):
    key_rows = jnp.concatenate([latent_cache, new_latent], axis=1)
    scores = (
        jnp.einsum("rshc,rjc->rshj", queries, key_rows, preferred_element_type=jnp.float32)
        * softmax_scale
    )
    cache_rows = latent_cache.shape[1]
    column = jnp.arange(cache_rows + 2, dtype=jnp.int32)
    step_ids = jnp.arange(2, dtype=jnp.int32)
    visible = (column[None, None, :] < cache_len[:, None, None]) | (
        column[None, None, :] == cache_rows
    )
    visible = visible | (column[None, None, :] == cache_rows + 1) & (step_ids[None, :, None] == 1)
    scores = jnp.where(visible[:, :, None, :], scores, excluded)
    row_max = jnp.max(scores, axis=-1, keepdims=True)
    exp_scores = jnp.exp(scores - row_max)
    weights_bf = (exp_scores / jnp.sum(exp_scores, axis=-1, keepdims=True)).astype(jnp.bfloat16)
    context = jnp.einsum(
        "rshj,rjc->rshc", weights_bf, key_rows[:, :, :LATENT], preferred_element_type=jnp.float32
    )
    return context.astype(jnp.bfloat16)


def local(
    tokens,
    router_logits,
    expert_ids,
    gate_up,
    down_proj,
    latent_cache,
    cache_len,
    new_latent,
    queries,
):
    experts = lax.axis_size("expert")
    tok_count, top_slots = expert_ids.shape
    model_width = tokens.shape[1]
    capacity = min(tok_count, max(2, tok_count * top_slots * 5 // (4 * experts)))
    slot_count = experts * capacity
    flat_ids = expert_ids.reshape(-1)
    onehot = (flat_ids[:, None] == jnp.arange(experts, dtype=jnp.int32)[None, :]).astype(jnp.int32)
    earlier = jnp.cumsum(onehot, axis=0) - onehot
    position = jnp.sum(earlier * onehot, axis=1)
    slot_index = flat_ids * capacity + position
    placed = slot_index[None, :] == jnp.arange(slot_count, dtype=jnp.int32)[:, None]
    chooser = jnp.any(placed.reshape(slot_count, tok_count, top_slots), axis=2).astype(jnp.bfloat16)
    outgoing = jnp.dot(chooser, tokens, preferred_element_type=jnp.float32).astype(jnp.bfloat16)
    arrived = lax.all_to_all(
        outgoing.reshape(experts, capacity, model_width),
        "expert",
        split_axis=0,
        concat_axis=0,
        tiled=True,
    )
    arrived = arrived.reshape(slot_count, model_width)
    gate_up_local = gate_up[0]
    down_local = down_proj[0]
    hidden = hidden_units(arrived, lax.all_gather(gate_up_local, "dp", axis=2, tiled=True))
    summed = jnp.dot(
        hidden,
        lax.all_gather(down_local, "dp", axis=0, tiled=True),
        preferred_element_type=jnp.float32,
    )
    returned = lax.all_to_all(
        summed.astype(jnp.bfloat16).reshape(experts, capacity, model_width),
        "expert",
        split_axis=0,
        concat_axis=0,
        tiled=True,
    )
    picked = returned.reshape(slot_count, model_width)[slot_index].reshape(
        tok_count, top_slots, model_width
    )
    gates = routing_gates(router_logits)
    mixed_tokens = jnp.sum(gates[:, :, None] * picked.astype(jnp.float32), axis=1).astype(
        jnp.bfloat16
    )
    context = latent_attention(latent_cache, cache_len, new_latent, queries)
    return (mixed_tokens, context)


def solution(mesh):
    return jax.shard_map(
        local,
        mesh=mesh,
        in_specs=(
            P(("groups", "expert", "dp"), None),
            P(("groups", "expert", "dp"), None),
            P(("groups", "expert", "dp"), None),
            P("expert", None, None, "dp"),
            P("expert", "dp", None),
            P(("groups", "expert", "dp"), None, None),
            P(("groups", "expert", "dp")),
            P(("groups", "expert", "dp"), None, None),
            P(("groups", "expert", "dp"), None, None, None),
        ),
        out_specs=(
            P(("groups", "expert", "dp"), None),
            P(("groups", "expert", "dp"), None, None, None),
        ),
        check_vma=False,
    )
```

profile of v0, /device:TPU:14, one launch (start us, length us, event | category | flops | bytes accessed | tf_op | source)
XLA Modules:
  0.0 282.2 jit_solution(6724271118250992053)
XLA Ops:
  7.2 0.0 copy-start
  7.2 0.0 copy-start.3
  7.2 0.0 all-gather.5.cloned.1.call-start
  7.2 0.7 all-gather.5.cloned.1.call-update
  7.9 0.0 copy-done.3
  7.9 0.1 copy.21
  8.0 0.1 eq.73
  8.1 0.1 eq.69
  8.2 1.2 reduce-window.6
  9.4 0.2 slice_reduce_fusion
  9.6 0.1 fusion.29
  9.7 0.1 reduce_sum.42
  9.8 0.5 fusion.13
  10.3 0.0 copy-done
  10.3 3.5 %convolution_convert_fusion = bf16[640,3584]{1,0:T(8,128)(2,1)} fusion(pred[640,64]{0,1:T(8,128)(4,1)S(1)} %fusion.13, bf16[64,3584]{1,0:T(8,128)(2,1)S(1)} %copy-done), kind=kOutput, calls=%fused_computation.8 | convolution fusion | flops 295895040 | bytes 5087232 | tf_op jit(solution)/shard_map/dot_general | solution.py:72
  13.9 7.1 %all-to-all-start = ((bf16[16,40,3584]{2,1,0:T(8,128)(2,1)}), bf16[16,40,3584]{2,1,0:T(8,128)(2,1)}, u32[]{:S(2)}, u32[]{:S(2)}) async-start(bf16[16,40,3584]{2,1,0:T(8,128)(2,1)} %bitcast.90), calls=%async_computation | async-start | bytes 9175040 | tf_op jit(solution)/shard_map/all_to_all | solution.py:73
  21.0 0.0 all-gather.7.cloned.1.call-start
  21.1 0.7 all-gather.7.cloned.1.call-update
  21.8 102.8 %all-to-all-done = bf16[16,40,3584]{2,1,0:T(8,128)(2,1)} async-done(((bf16[16,40,3584]{2,1,0:T(8,128)(2,1)}), bf16[16,40,3584]{2,1,0:T(8,128)(2,1)}, u32[]{:S(2)}, u32[]{:S(2)}) %all-to-all-start) | async-done | bytes 4587552 | tf_op jit(solution)/shard_map/all_to_all | solution.py:73
  124.6 0.0 all-gather.5.cloned.1.call-done
  124.6 15.9 %fusion.1 = f32[640,2,1024]{2,0,1:T(8,128)} fusion(bf16[640,3584,1]{1,0,2:T(8,128)(2,1)} %bitcast.3, bf16[1,2,3584,1024]{3,2,1,0:T(8,128)(2,1)} %all-gather.5.cloned.1.call-done), kind=kOutput, calls=%fused_computation.2 | convolution fusion | flops 9395240960 | bytes 24510464 | tf_op jit(solution)/shard_map/rd,gdf->rgf/dot_general | solution.py:20
  140.5 0.0 all-gather.7.cloned.1.call-done
  140.5 11.6 %fusion.6 = bf16[640,3584]{1,0:T(8,128)(2,1)} fusion(bf16[1,1024,3584]{2,1,0:T(8,128)(2,1)} %all-gather.7.cloned.1.call-done, f32[640,2,1024]{2,0,1:T(8,128)} %fusion.1), kind=kOutput, calls=%fused_computation.9 | convolution fusion | flops 4703846400 | bytes 17170432 | tf_op jit(solution)/shard_map/dot_general | solution.py:84
  152.1 0.0 copy-start.2
  152.1 0.0 copy-start.1
  152.2 0.0 copy-start.4
  152.2 0.0 copy-start.5
  152.2 5.3 %all-to-all-start.1 = ((bf16[16,40,3584]{2,1,0:T(8,128)(2,1)}), bf16[16,40,3584]{2,1,0:T(8,128)(2,1)}, u32[]{:S(2)}, u32[]{:S(2)}) async-start(bf16[16,40,3584]{2,1,0:T(8,128)(2,1)} %bitcast.91), calls=%async_computation.1 | async-start | bytes 9175040 | tf_op jit(solution)/shard_map/all_to_all | solution.py:89
  157.4 0.1 mul.62
  157.5 0.0 copy-done.2
  157.6 0.1 copy.20
  158.3 0.0 copy-done.1
  158.3 0.3 copy.25
  158.7 0.1 and_or_fusion
  158.8 0.0 copy-done.4
  158.8 0.0 copy-done.5
  158.8 0.5 fusion.50
  159.3 1.1 fusion.18
  160.4 98.4 %all-to-all-done.1 = bf16[16,40,3584]{2,1,0:T(8,128)(2,1)} async-done(((bf16[16,40,3584]{2,1,0:T(8,128)(2,1)}), bf16[16,40,3584]{2,1,0:T(8,128)(2,1)}, u32[]{:S(2)}, u32[]{:S(2)}) %all-to-all-start.1) | async-done | bytes 4587552 | tf_op jit(solution)/shard_map/all_to_all | solution.py:89
  258.8 10.8 %gather_fusion = bf16[512,3584]{1,0:T(8,128)(2,1)} fusion(bf16[640,3584]{1,0:T(8,128)(2,1)} %bitcast.9, s32[1024]{0:T(1024)S(1)} %pad_clamp_fusion), kind=kCustom, calls=%fused_computation | custom fusion | bytes 7342080 | tf_op jit(solution)/shard_map/gather | solution.py:96
  269.6 5.8 %fusion.3 = bf16[64,3584]{1,0:T(8,128)(2,1)} fusion(bf16[512,3584]{1,0:T(8,128)(2,1)} %gather_fusion, f32[64,8]{1,0:T(8,128)S(1)} %copy.20), kind=kLoop, calls=%fused_computation.5 | loop fusion | flops 5275648 | bytes 4130816 | tf_op jit(solution)/shard_map/reduce_sum | solution.py:100
  (10 shorter events, 0.1 us)
Async XLA Ops:
  7.2 3.1 %copy-start = (bf16[64,3584]{1,0:T(8,128)(2,1)S(1)}, bf16[64,3584]{1,0:T(8,128)(2,1)}, u32[]{:S(2)}) copy-start(bf16[64,3584]{1,0:T(8,128)(2,1)} %param.9) | copy-start | bytes 1376260
  7.2 0.7 copy-start.3
  7.2 117.4 %all-gather.5.cloned.1.call-start = ((), (), s32[]{:S(2)}) async-start(), calls=%async_computation.2 | async-start | bytes 22020096 | tf_op jit(solution)/shard_map/all_gather | solution.py:83
  13.9 110.7 %all-to-all-start = ((bf16[16,40,3584]{2,1,0:T(8,128)(2,1)}), bf16[16,40,3584]{2,1,0:T(8,128)(2,1)}, u32[]{:S(2)}, u32[]{:S(2)}) async-start(bf16[16,40,3584]{2,1,0:T(8,128)(2,1)} %bitcast.90), calls=%async_computation | async-start | bytes 9175040 | tf_op jit(solution)/shard_map/all_to_all | solution.py:73
  21.0 119.5 %all-gather.7.cloned.1.call-start = ((), (), s32[]{:S(2)}) async-start(), calls=%async_computation.3 | async-start | bytes 11010048 | tf_op jit(solution)/shard_map/all_gather | solution.py:86
  152.1 5.4 %copy-start.2 = (f32[64,8]{0,1:T(8,128)S(1)}, f32[64,8]{0,1:T(8,128)}, u32[]{:S(2)}) copy-start(f32[64,8]{0,1:T(8,128)} %param.10) | copy-start | bytes 6148
  152.1 6.2 %copy-start.1 = (bf16[1,512,576]{1,2,0:T(8,128)(2,1)S(1)}, bf16[1,512,576]{1,2,0:T(8,128)(2,1)}, u32[]{:S(2)}) copy-start(bf16[1,512,576]{1,2,0:T(8,128)(2,1)} %param.14) | copy-start | bytes 1769476
  152.2 6.6 %copy-start.4 = (bf16[1,2,128,576]{2,3,1,0:T(8,128)(2,1)S(1)}, bf16[1,2,128,576]{2,3,1,0:T(8,128)(2,1)}, u32[]{:S(2)}) copy-start(bf16[1,2,128,576]{2,3,1,0:T(8,128)(2,1)} %param.17) | copy-start | bytes 884740
  152.2 6.6 %copy-start.5 = (bf16[1,2,576]{2,1,0:T(2,128)(2,1)S(1)}, bf16[1,2,576]{2,1,0:T(2,128)(2,1)}, u32[]{:S(2)}) copy-start(bf16[1,2,576]{2,1,0:T(2,128)(2,1)} %param.16) | copy-start | bytes 6916
  152.2 106.6 %all-to-all-start.1 = ((bf16[16,40,3584]{2,1,0:T(8,128)(2,1)}), bf16[16,40,3584]{2,1,0:T(8,128)(2,1)}, u32[]{:S(2)}, u32[]{:S(2)}) async-start(bf16[16,40,3584]{2,1,0:T(8,128)(2,1)} %bitcast.91), calls=%async_computation.1 | async-start | bytes 9175040 | tf_op jit(solution)/shard_map/all_to_all | solution.py:89
Sparse Core Ops, SparseCore 0:
  9.6 28.3 all-gather.4
  39.5 19.4 all-gather.6
where the time goes:
time: 283 us; the launch traced here: 282 us
  waiting for transfers between devices  203 us (72%)
  matrix products  32.8 us (12%)
  between operations  14.8 us (5%)
  starting transfers between devices  12.5 us (4%)
  local copies, waits for them, and re-layouts  11.9 us (4%)
  other arithmetic  7.72 us (3%)
    all_to_all x1, waiting for transfers between devices, local(): lax.all_to_all(outgoing.reshape(experts, capacity, model_width), 'expert'...  103 us
    all_to_all x1, waiting for transfers between devices, local(): lax.all_to_all(summed.astype(jnp.bfloat16).reshape(experts, capacity, mod...  98.4 us
    dot_general x1, matrix products, hidden_units(): jnp.einsum('rd,gdf->rgf', row_block, gate_up_half, preferred_element_type...  15.9 us
    dot_general x1, matrix products, local(): jnp.dot(hidden, lax.all_gather(down_local, 'dp', axis=0, tiled=True), pre...  11.6 us
    gather x1, local copies, waits for them, and re-layouts, local(): returned.reshape(slot_count, model_width)[slot_index]  10.8 us
    all_to_all x1, starting transfers between devices, local(): lax.all_to_all(outgoing.reshape(experts, capacity, model_width), 'expert'...  7.14 us
    reduce_sum x1, other arithmetic, local(): jnp.sum(gates[:, :, None] * picked.astype(jnp.float32), axis=1)  5.82 us
  transfers between devices with their start and end apart: 4, of which 2 were waited for; matrix products, arithmetic and copies ran while one was open for 9% of the time, Pallas kernels for 0%

commit v1 on v0

--- a/solution.py
+++ b/solution.py
@@ -1,6 +1,8 @@
 import jax
 import jax.numpy as jnp
 from jax import lax
+from jax.experimental import pallas as pl
+from jax.experimental.pallas import tpu as pltpu
 from jax.sharding import PartitionSpec as P
 
 LATENT = 512
@@ -104,9 +106,272 @@
     return (mixed_tokens, context)
 
 
+AUX = 128
+
+
+def partners():
+    me = lax.axis_index("expert")
+    x, y, z = me % 2, (me // 2) % 2, me // 4
+    plane = me % 4
+    x_next = me + 1 - 2 * x
+    y_next = me + 2 - 4 * y
+    along_z = [(z + 1 - 2 * (z % 2)) * 4 + plane, (3 - z) * 4 + plane, ((z + 2) % 4) * 4 + plane]
+    return me, x_next, y_next, along_z
+
+
+def attend(q_ref, cache_ref, len_ref, new_ref, ctx_ref):
+    q = q_ref[...]
+    rows, keys = q.shape[0], cache_ref.shape[0]
+    scores = softmax_scale * lax.dot_general(
+        q, cache_ref[...], (((1,), (1,)), ((), ())), preferred_element_type=jnp.float32
+    )
+    column = lax.broadcasted_iota(jnp.int32, (rows, keys), 1)
+    scores = jnp.where(column < len_ref[0], scores, excluded)
+    new = new_ref[...].astype(jnp.float32)
+    qf = q.astype(jnp.float32)
+    first = softmax_scale * jnp.sum(qf * new[0:1], axis=1, keepdims=True)
+    second = softmax_scale * jnp.sum(qf * new[1:2], axis=1, keepdims=True)
+    row = lax.broadcasted_iota(jnp.int32, (rows, 1), 0)
+    second = jnp.where(row >= rows // 2, second, excluded)
+    top = jnp.maximum(jnp.max(scores, axis=1, keepdims=True), jnp.maximum(first, second))
+    e, e1, e2 = jnp.exp(scores - top), jnp.exp(first - top), jnp.exp(second - top)
+    total = jnp.sum(e, axis=1, keepdims=True) + e1 + e2
+    p = (e / total).astype(jnp.bfloat16)
+    p1 = (e1 / total).astype(jnp.bfloat16).astype(jnp.float32)
+    p2 = (e2 / total).astype(jnp.bfloat16).astype(jnp.float32)
+    ctx = jnp.dot(p, cache_ref[:, :LATENT], preferred_element_type=jnp.float32)
+    ctx = ctx + p1 * new[0:1, :LATENT] + p2 * new[1:2, :LATENT]
+    ctx_ref[...] = ctx.astype(ctx_ref.dtype)
+
+
+def layer_kernel(
+    tok_ref, log_ref, ids_ref, gu_ref, dn_ref, cache_ref, len_ref, new_ref, q_ref,
+    out_ref, ctx_ref,
+    xs, gu, dn, hid, part, r1x, r1y, r2x, r2y, r3,
+    send_sem, recv_sem, local_sem,
+):
+    group, core = lax.axis_index("groups"), lax.axis_index("dp")
+    me, x_next, y_next, along_z = partners()
+    rows, width = tok_ref.shape
+    half = rows // 2
+    ffh = gu_ref.shape[2]
+    mine = lambda e: (group, e, core)
+    x_dev, y_dev = mine(x_next), mine(y_next)
+    z_dev = [None] + [mine(e) for e in along_z]
+    core_dev = (group, me, 1 - core)
+    count = [0]
+    sent = []
+
+    def send(src, dst, dev):
+        k = count[0]
+        count[0] += 1
+        copy = pltpu.make_async_remote_copy(
+            src_ref=src, dst_ref=dst, send_sem=send_sem.at[k], recv_sem=recv_sem.at[k],
+            device_id=dev, device_id_type=pl.DeviceIdType.MESH,
+        )
+        copy.start()
+        sent.append(copy)
+        return copy
+
+    load = pltpu.make_async_copy(tok_ref, xs.at[0, pl.ds(0, rows), pl.ds(0, width)], local_sem.at[0])
+    load.start()
+    own_gu = pltpu.make_async_copy(gu_ref, gu.at[0], local_sem.at[1])
+    own_dn = pltpu.make_async_copy(dn_ref, dn.at[pl.ds(0, ffh)], local_sem.at[2])
+
+    barrier = pltpu.get_barrier_semaphore()
+    greet = [x_dev, y_dev, z_dev[1], z_dev[2], z_dev[3], core_dev]
+    for dev in greet:
+        pl.semaphore_signal(barrier, inc=1, device_id=dev, device_id_type=pl.DeviceIdType.MESH)
+
+    experts = lax.axis_size("expert")
+    affinity = jax.nn.sigmoid(log_ref[...])
+    gates = route_scale * affinity / jnp.sum(affinity, axis=1, keepdims=True)
+    ids = ids_ref[...]
+    lane = lax.broadcasted_iota(jnp.int32, (rows, AUX), 1)
+    named = jnp.where(lane < experts, lane, lane - experts)
+    weight = jnp.zeros((rows, AUX), jnp.float32)
+    for k in range(ids.shape[1]):
+        weight = weight + jnp.where(ids[:, k : k + 1] == named, gates[:, k : k + 1], 0.0)
+    high = weight.astype(jnp.bfloat16).astype(jnp.float32)
+    packed = jnp.where(lane < experts, high, jnp.where(lane < 2 * experts, weight - high, 0.0))
+    xs[0, pl.ds(0, rows), pl.ds(width, AUX)] = packed.astype(jnp.bfloat16)
+
+    pl.semaphore_wait(barrier, len(greet))
+    load.wait()
+
+    def block(i, g, lo=0, size=None):
+        return xs.at[i, pl.ds(g * rows + lo, rows if size is None else size)]
+
+    def piece(i, g, lo=0, size=None):
+        return part.at[i, pl.ds(g * rows + lo, rows if size is None else size)]
+
+    gx, gy, gz, fx, fy = {}, {}, {}, {}, {}
+    gx[0] = send(block(0, 0), block(0, 1), x_dev)
+    gy[0] = send(block(0, 0), block(0, 2), y_dev)
+    for i in (1, 2, 3):
+        gz[i] = send(block(0, 0), block(i, 0), z_dev[i])
+    peer_gu = send(gu_ref, gu.at[1], core_dev)
+    peer_dn = send(dn_ref, dn.at[pl.ds(ffh, ffh)], core_dev)
+    own_gu.start()
+    own_dn.start()
+
+    attend(q_ref, cache_ref, len_ref, new_ref, ctx_ref)
+
+    def forward(i):
+        gx[i].wait_recv()
+        fy[i] = send(block(i, 1, 0, half), block(i, 3, 0, half), y_dev)
+        gy[i].wait_recv()
+        fx[i] = send(block(i, 2, half, half), block(i, 3, half, half), x_dev)
+
+    def spread(i):
+        gz[i].wait_recv()
+        gx[i] = send(block(i, 0), block(i, 1), x_dev)
+        gy[i] = send(block(i, 0), block(i, 2), y_dev)
+
+    tile_f, tile_d = 256, 512
+
+    def compute(i):
+        fy[i].wait_recv()
+        fx[i].wait_recv()
+        if i == 0:
+            own_gu.wait()
+            own_dn.wait()
+            peer_gu.wait_recv()
+            peer_dn.wait_recv()
+        per = ffh // tile_f
+
+        def up(j, carry):
+            c = j // per
+            cols = pl.ds(pl.multiple_of((j % per) * tile_f, tile_f), tile_f)
+            x = xs[i, :, pl.ds(0, width)]
+            g = jnp.dot(x, gu[c, 0, :, cols], preferred_element_type=jnp.float32)
+            u = jnp.dot(x, gu[c, 1, :, cols], preferred_element_type=jnp.float32)
+            h = g / (1.0 + jnp.exp(-g)) * u
+            hid[:, pl.ds(pl.multiple_of(j * tile_f, tile_f), tile_f)] = h.astype(jnp.bfloat16)
+            return carry
+
+        lax.fori_loop(0, 2 * per, up, 0)
+        aux = xs[i, :, pl.ds(width, AUX)].astype(jnp.float32)
+        lanes = lax.broadcasted_iota(jnp.int32, aux.shape, 1)
+        chosen = (lanes == me) | (lanes == me + experts)
+        w = jnp.sum(jnp.where(chosen, aux, 0.0), axis=1, keepdims=True)
+
+        def down(j, carry):
+            cols = pl.ds(pl.multiple_of(j * tile_d, tile_d), tile_d)
+            o = jnp.dot(hid[...], dn[:, cols], preferred_element_type=jnp.float32)
+            part[i, :, cols] = (o * w).astype(jnp.bfloat16)
+            return carry
+
+        lax.fori_loop(0, width // tile_d, down, 0)
+
+    def add(ref, others, lo=0):
+        total = ref[...].astype(jnp.float32)
+        for other in others:
+            total = total + other[...].astype(jnp.float32)
+        return total.astype(jnp.bfloat16)
+
+    d1x, d1y, d2x, d2y, d2xb, d2yb, d3 = {}, {}, {}, {}, {}, {}, {}
+
+    def step1(i):
+        d1x[i] = send(piece(i, 3, 0, half), r1x.at[i], x_dev)
+        d1y[i] = send(piece(i, 3, half, half), r1y.at[i], y_dev)
+        d2x[i] = send(piece(i, 1, 0, half), r2x.at[i, pl.ds(0, half)], x_dev)
+        d2y[i] = send(piece(i, 2, half, half), r2y.at[i, pl.ds(half, half)], y_dev)
+
+    def step2(i):
+        d1x[i].wait_recv()
+        spot = piece(i, 2, 0, half)
+        spot[...] = add(spot, [r1x.at[i]])
+        d2yb[i] = send(spot, r2y.at[i, pl.ds(0, half)], y_dev)
+        d1y[i].wait_recv()
+        spot = piece(i, 1, half, half)
+        spot[...] = add(spot, [r1y.at[i]])
+        d2xb[i] = send(spot, r2x.at[i, pl.ds(half, half)], x_dev)
+
+    def step3(i):
+        for d in (d2x, d2y, d2xb, d2yb):
+            d[i].wait_recv()
+        if i > 0:
+            spot = piece(i, 0)
+            spot[...] = add(spot, [r2x.at[i], r2y.at[i]])
+            d3[i] = send(spot, r3.at[i - 1], z_dev[i])
+
+    forward(0)
+    spread(1)
+    compute(0)
+    step1(0)
+    forward(1)
+    spread(2)
+    compute(1)
+    step1(1)
+    step2(0)
+    forward(2)
+    spread(3)
+    compute(2)
+    step1(2)
+    step2(1)
+    forward(3)
+    step3(0)
+    compute(3)
+    step1(3)
+    step2(2)
+    step3(1)
+    step2(3)
+    step3(2)
+    step3(3)
+    for i in (1, 2, 3):
+        d3[i].wait_recv()
+    out_ref[...] = add(piece(0, 0), [r2x.at[0], r2y.at[0], r3.at[0], r3.at[1], r3.at[2]])
+    for copy in sent:
+        copy.wait_send()
+
+
+def local_kernel(
+    tokens, router_logits, expert_ids, gate_up, down_proj, latent_cache, cache_len, new_latent, queries
+):
+    rows, width = tokens.shape
+    ffh = gate_up.shape[3]
+    bf = jnp.bfloat16
+    q = queries.reshape(-1, queries.shape[-1])
+    vmem = pl.BlockSpec(memory_space=pltpu.VMEM)
+    hbm = pl.BlockSpec(memory_space=pl.ANY)
+    mixed, ctx = pl.pallas_call(
+        layer_kernel,
+        out_shape=(
+            jax.ShapeDtypeStruct((rows, width), bf),
+            jax.ShapeDtypeStruct((q.shape[0], LATENT), bf),
+        ),
+        in_specs=[hbm, vmem, vmem, hbm, hbm, vmem, pl.BlockSpec(memory_space=pltpu.SMEM), vmem, vmem],
+        out_specs=(vmem, vmem),
+        scratch_shapes=[
+            pltpu.VMEM((4, 4 * rows, width + AUX), bf),
+            pltpu.VMEM((2, 2, width, ffh), bf),
+            pltpu.VMEM((2 * ffh, width), bf),
+            pltpu.VMEM((4 * rows, 2 * ffh), bf),
+            pltpu.VMEM((4, 4 * rows, width), bf),
+            pltpu.VMEM((4, rows // 2, width), bf),
+            pltpu.VMEM((4, rows // 2, width), bf),
+            pltpu.VMEM((4, rows, width), bf),
+            pltpu.VMEM((4, rows, width), bf),
+            pltpu.VMEM((3, rows, width), bf),
+            pltpu.SemaphoreType.DMA((64,)),
+            pltpu.SemaphoreType.DMA((64,)),
+            pltpu.SemaphoreType.DMA((3,)),
+        ],
+        compiler_params=pltpu.CompilerParams(
+            collective_id=0, has_side_effects=True, vmem_limit_bytes=60 * 1024 * 1024
+        ),
+    )(
+        tokens, router_logits, expert_ids, gate_up[0], down_proj[0], latent_cache[0], cache_len,
+        new_latent[0], q,
+    )
+    return mixed, ctx.reshape(queries.shape[:3] + (LATENT,))
+
+
 def solution(mesh):
+    whole = mesh.shape["expert"] == 16 and mesh.shape["dp"] == 2
     return jax.shard_map(
-        local,
+        local_kernel if whole else local,
         mesh=mesh,
         in_specs=(
             P(("groups", "expert", "dp"), None),

time: 283 us -> 183 us (0.65)
  the two profiles are of different devices: /device:TPU:14 before, /device:TPU:0 now
where the time goes in v1:
time: 183 us
  Pallas kernels  171 us (93%)
  local copies, waits for them, and re-layouts  10.3 us (6%)
    pallas_call x1, Pallas kernels, local_kernel(): pl.pallas_call(layer_kernel, out_shape=(jax.ShapeDtypeStruct((rows, width...  171 us
    unnamed x6, local copies, waits for them, and re-layouts  10.3 us

profile of v1, /device:TPU:0, one launch (start us, length us, event | category | flops | bytes accessed | tf_op | source)
XLA Modules:
  0.0 182.5 jit_solution(13147000806861326999)
XLA Ops:
  1.3 1.4 copy.13.log_ref
  2.7 1.4 copy.14.ids_ref
  4.0 1.9 %copy.12 = bf16[1,2,128,576]{3,2,1,0:T(8,128)(2,1)} copy(bf16[1,2,128,576]{2,3,1,0:T(8,128)(2,1)} %param.17) | data formatting | bytes 589824 | tf_op args[8]
  5.9 2.2 %copy.11 = bf16[1,512,576]{2,1,0:T(8,128)(2,1)} copy(bf16[1,512,576]{1,2,0:T(8,128)(2,1)} %param.14) | data formatting | bytes 1179648 | tf_op args[5]
  8.1 171.0 %shard_map.104 = (bf16[64,3584]{1,0:T(8,128)(2,1)}, bf16[256,512]{1,0:T(8,128)(2,1)}) custom-call(bf16[64,3584]{1,0:T(8,128)(2,1)} %tok_ref.1, f32[64,8]{1,0:T(8,128)} %copy.13.log_ref, s32[64,8]{1,0:T(8,128)} %copy.14.ids_ref, bf16[2,3584,512]{2,1,0:T(8,128)(2,1)} %bitcast.6, bf16[512,3584]{1,0:T(8,128)(2,1)} %bitcast.7, bf16[512,576]{1,0:T(8,128)(2,1)} %bitcast.8, ...), custom_call_target="tpu_custom_call" | custom-call | tf_op jit(solution)/shard_map/pallas_call | solution.py:338
  179.1 1.8 copy.18
  180.9 1.7 copy.19

commit v2 on v1

--- a/solution.py
+++ b/solution.py
@@ -115,33 +115,41 @@
     plane = me % 4
     x_next = me + 1 - 2 * x
     y_next = me + 2 - 4 * y
-    along_z = [(z + 1 - 2 * (z % 2)) * 4 + plane, (3 - z) * 4 + plane, ((z + 2) % 4) * 4 + plane]
-    return me, x_next, y_next, along_z
+    inner = ((z + 1) // 2) % 2
+    mirror, second = 3 - z, (z + 2) % 4
+    along_z = [
+        (z + 1 - 2 * (z % 2)) * 4 + plane,
+        (inner * mirror + (1 - inner) * second) * 4 + plane,
+        (inner * second + (1 - inner) * mirror) * 4 + plane,
+    ]
+    return me, x_next, y_next, along_z, inner
 
 
 def attend(q_ref, cache_ref, len_ref, new_ref, ctx_ref):
-    q = q_ref[...]
-    rows, keys = q.shape[0], cache_ref.shape[0]
-    scores = softmax_scale * lax.dot_general(
-        q, cache_ref[...], (((1,), (1,)), ((), ())), preferred_element_type=jnp.float32
-    )
-    column = lax.broadcasted_iota(jnp.int32, (rows, keys), 1)
-    scores = jnp.where(column < len_ref[0], scores, excluded)
-    new = new_ref[...].astype(jnp.float32)
-    qf = q.astype(jnp.float32)
-    first = softmax_scale * jnp.sum(qf * new[0:1], axis=1, keepdims=True)
-    second = softmax_scale * jnp.sum(qf * new[1:2], axis=1, keepdims=True)
-    row = lax.broadcasted_iota(jnp.int32, (rows, 1), 0)
-    second = jnp.where(row >= rows // 2, second, excluded)
-    top = jnp.maximum(jnp.max(scores, axis=1, keepdims=True), jnp.maximum(first, second))
-    e, e1, e2 = jnp.exp(scores - top), jnp.exp(first - top), jnp.exp(second - top)
-    total = jnp.sum(e, axis=1, keepdims=True) + e1 + e2
-    p = (e / total).astype(jnp.bfloat16)
-    p1 = (e1 / total).astype(jnp.bfloat16).astype(jnp.float32)
-    p2 = (e2 / total).astype(jnp.bfloat16).astype(jnp.float32)
-    ctx = jnp.dot(p, cache_ref[:, :LATENT], preferred_element_type=jnp.float32)
-    ctx = ctx + p1 * new[0:1, :LATENT] + p2 * new[1:2, :LATENT]
-    ctx_ref[...] = ctx.astype(ctx_ref.dtype)
+    keys, heads = cache_ref.shape[1], q_ref.shape[2]
+    new = new_ref[...]
+    for step in range(2):
+        q = q_ref[step]
+        scores = softmax_scale * lax.dot_general(
+            cache_ref[...], q, (((0,), (0,)), ((), ())), preferred_element_type=jnp.float32
+        )
+        position = lax.broadcasted_iota(jnp.int32, (keys, heads), 0)
+        scores = jnp.where(position < len_ref[0], scores, excluded)
+        fresh = softmax_scale * jnp.dot(new, q, preferred_element_type=jnp.float32)
+        which = lax.broadcasted_iota(jnp.int32, fresh.shape, 0)
+        fresh = jnp.where(which <= step, fresh, excluded)
+        top = jnp.maximum(
+            jnp.max(scores, axis=0, keepdims=True), jnp.max(fresh, axis=0, keepdims=True)
+        )
+        e, e_new = jnp.exp(scores - top), jnp.exp(fresh - top)
+        total = jnp.sum(e, axis=0, keepdims=True) + jnp.sum(e_new, axis=0, keepdims=True)
+        p = (e / total).astype(jnp.bfloat16)
+        p_new = (e_new / total).astype(jnp.bfloat16)
+        ctx = jnp.dot(cache_ref[:LATENT], p, preferred_element_type=jnp.float32).T
+        ctx = ctx + lax.dot_general(
+            p_new, new[:, :LATENT], (((0,), (0,)), ((), ())), preferred_element_type=jnp.float32
+        )
+        ctx_ref[step] = ctx.astype(ctx_ref.dtype)
 
 
 def layer_kernel(
@@ -151,7 +159,7 @@
     send_sem, recv_sem, local_sem,
 ):
     group, core = lax.axis_index("groups"), lax.axis_index("dp")
-    me, x_next, y_next, along_z = partners()
+    me, x_next, y_next, along_z, inner = partners()
     rows, width = tok_ref.shape
     half = rows // 2
     ffh = gu_ref.shape[2]
@@ -162,13 +170,17 @@
     count = [0]
     sent = []
 
-    def send(src, dst, dev):
+    def plan(src, dst, dev, arrival=None):
         k = count[0]
         count[0] += 1
-        copy = pltpu.make_async_remote_copy(
-            src_ref=src, dst_ref=dst, send_sem=send_sem.at[k], recv_sem=recv_sem.at[k],
+        return pltpu.make_async_remote_copy(
+            src_ref=src, dst_ref=dst, send_sem=send_sem.at[k],
+            recv_sem=recv_sem.at[k if arrival is None else arrival],
             device_id=dev, device_id_type=pl.DeviceIdType.MESH,
         )
+
+    def send(src, dst, dev, arrival=None):
+        copy = plan(src, dst, dev, arrival)
         copy.start()
         sent.append(copy)
         return copy
@@ -185,16 +197,16 @@
 
     experts = lax.axis_size("expert")
     affinity = jax.nn.sigmoid(log_ref[...])
-    gates = route_scale * affinity / jnp.sum(affinity, axis=1, keepdims=True)
+    gates = route_scale * affinity / jnp.sum(affinity, axis=0, keepdims=True)
     ids = ids_ref[...]
-    lane = lax.broadcasted_iota(jnp.int32, (rows, AUX), 1)
+    lane = lax.broadcasted_iota(jnp.int32, (AUX, rows), 0)
     named = jnp.where(lane < experts, lane, lane - experts)
-    weight = jnp.zeros((rows, AUX), jnp.float32)
-    for k in range(ids.shape[1]):
-        weight = weight + jnp.where(ids[:, k : k + 1] == named, gates[:, k : k + 1], 0.0)
+    weight = jnp.zeros((AUX, rows), jnp.float32)
+    for k in range(ids.shape[0]):
+        weight = weight + jnp.where(ids[k : k + 1] == named, gates[k : k + 1], 0.0)
     high = weight.astype(jnp.bfloat16).astype(jnp.float32)
     packed = jnp.where(lane < experts, high, jnp.where(lane < 2 * experts, weight - high, 0.0))
-    xs[0, pl.ds(0, rows), pl.ds(width, AUX)] = packed.astype(jnp.bfloat16)
+    xs[0, pl.ds(0, rows), pl.ds(width, AUX)] = packed.T.astype(jnp.bfloat16)
 
     pl.semaphore_wait(barrier, len(greet))
     load.wait()
@@ -205,11 +217,21 @@
     def piece(i, g, lo=0, size=None):
         return part.at[i, pl.ds(g * rows + lo, rows if size is None else size)]
 
-    gx, gy, gz, fx, fy = {}, {}, {}, {}, {}
+    gx, gy, fx, fy = {}, {}, {}, {}
+    inside, outside = inner == 1, inner == 0
+    arrivals = {1: 58, 2: 59, 3: 60}
     gx[0] = send(block(0, 0), block(0, 1), x_dev)
     gy[0] = send(block(0, 0), block(0, 2), y_dev)
-    for i in (1, 2, 3):
-        gz[i] = send(block(0, 0), block(i, 0), z_dev[i])
+    hop1 = send(block(0, 0), block(1, 0), z_dev[1], arrivals[1])
+    hop2 = plan(block(0, 0), block(2, 0), z_dev[2], arrivals[2])
+    on_far = plan(block(1, 0), block(3, 0), z_dev[2], arrivals[3])
+    on_near = plan(block(2, 0), block(2, 0), z_dev[1], arrivals[2])
+    on_last = plan(block(3, 0), block(3, 0), z_dev[1], arrivals[3])
+
+    @pl.when(inside)
+    def _():
+        hop2.start()
+
     peer_gu = send(gu_ref, gu.at[1], core_dev)
     peer_dn = send(dn_ref, dn.at[pl.ds(ffh, ffh)], core_dev)
     own_gu.start()
@@ -224,7 +246,6 @@
         fx[i] = send(block(i, 2, half, half), block(i, 3, half, half), x_dev)
 
     def spread(i):
-        gz[i].wait_recv()
         gx[i] = send(block(i, 0), block(i, 1), x_dev)
         gy[i] = send(block(i, 0), block(i, 2), y_dev)
 
@@ -270,7 +291,7 @@
             total = total + other[...].astype(jnp.float32)
         return total.astype(jnp.bfloat16)
 
-    d1x, d1y, d2x, d2y, d2xb, d2yb, d3 = {}, {}, {}, {}, {}, {}, {}
+    d1x, d1y, d2x, d2y, d2xb, d2yb = {}, {}, {}, {}, {}, {}
 
     def step1(i):
         d1x[i] = send(piece(i, 3, 0, half), r1x.at[i], x_dev)
@@ -294,36 +315,65 @@
         if i > 0:
             spot = piece(i, 0)
             spot[...] = add(spot, [r2x.at[i], r2y.at[i]])
-            d3[i] = send(spot, r3.at[i - 1], z_dev[i])
-
+            slot = {1: 0, 2: 2 - inner, 3: 1 + inner}[i]
+            send(spot, r3.at[slot], z_dev[i], 61 + slot)
+
+    hop1.wait_recv()
+
+    @pl.when(inside)
+    def _():
+        on_far.start()
+
+    spread(1)
     forward(0)
-    spread(1)
+    hop2.wait_recv()
+
+    @pl.when(inside)
+    def _():
+        on_near.start()
+
+    spread(2)
+
+    @pl.when(inside)
+    def _():
+        on_far.wait_recv()
+        on_last.start()
+
     compute(0)
-    step1(0)
     forward(1)
-    spread(2)
+
+    @pl.when(outside)
+    def _():
+        on_last.wait_recv()
+
+    spread(3)
     compute(1)
-    step1(1)
-    step2(0)
     forward(2)
-    spread(3)
     compute(2)
     step1(2)
-    step2(1)
     forward(3)
-    step3(0)
+    step1(1)
+    step2(2)
     compute(3)
     step1(3)
-    step2(2)
+    step3(2)
+    step2(1)
+    step2(3)
+    step1(0)
     step3(1)
-    step2(3)
-    step3(2)
     step3(3)
-    for i in (1, 2, 3):
-        d3[i].wait_recv()
+    step2(0)
+    step3(0)
+    for slot in range(3):
+        plan(piece(0, 0), r3.at[slot], z_dev[1], 61 + slot).wait_recv()
     out_ref[...] = add(piece(0, 0), [r2x.at[0], r2y.at[0], r3.at[0], r3.at[1], r3.at[2]])
     for copy in sent:
         copy.wait_send()
+
+    @pl.when(inside)
+    def _():
+        for copy in (hop2, on_far, on_near, on_last):
+            copy.wait_send()
 
 
 def local_kernel(
@@ -332,14 +382,14 @@
     rows, width = tokens.shape
     ffh = gate_up.shape[3]
     bf = jnp.bfloat16
-    q = queries.reshape(-1, queries.shape[-1])
+    q = queries[0].swapaxes(1, 2)
     vmem = pl.BlockSpec(memory_space=pltpu.VMEM)
     hbm = pl.BlockSpec(memory_space=pl.ANY)
     mixed, ctx = pl.pallas_call(
         layer_kernel,
         out_shape=(
             jax.ShapeDtypeStruct((rows, width), bf),
-            jax.ShapeDtypeStruct((q.shape[0], LATENT), bf),
+            jax.ShapeDtypeStruct(queries.shape[1:3] + (LATENT,), bf),
         ),
         in_specs=[hbm, vmem, vmem, hbm, hbm, vmem, pl.BlockSpec(memory_space=pltpu.SMEM), vmem, vmem],
         out_specs=(vmem, vmem),
@@ -362,10 +412,10 @@
             collective_id=0, has_side_effects=True, vmem_limit_bytes=60 * 1024 * 1024
         ),
     )(
-        tokens, router_logits, expert_ids, gate_up[0], down_proj[0], latent_cache[0], cache_len,
+        tokens, router_logits.T, expert_ids.T, gate_up[0], down_proj[0], latent_cache[0].T, cache_len,
         new_latent[0], q,
     )
-    return mixed, ctx.reshape(queries.shape[:3] + (LATENT,))
+    return mixed, ctx[None]
 
 
 def solution(mesh):

time: 183 us -> 154 us (0.84)
  Pallas kernels: 171 us -> 149 us
  local copies, waits for them, and re-layouts: 10.3 us -> 3.48 us
    pallas_call x1, Pallas kernels: 171 us -> 149 us  [local_kernel(): pl.pallas_call(layer_kernel, out_shape=(jax.ShapeDtypeStruct((rows, width...]
    unnamed x6 -> x2, local copies, waits for them, and re-layouts: 10.3 us -> 3.48 us
where the time goes in v2:
time: 154 us; the launch traced here: 153 us
  Pallas kernels  149 us (97%)
  local copies, waits for them, and re-layouts  3.48 us (2%)
    pallas_call x1, Pallas kernels, local_kernel(): pl.pallas_call(layer_kernel, out_shape=(jax.ShapeDtypeStruct((rows, width...  149 us
    unnamed x2, local copies, waits for them, and re-layouts  3.48 us

profile of v2, /device:TPU:0, one launch (start us, length us, event | category | flops | bytes accessed | tf_op | source)
XLA Modules:
  0.0 153.4 jit_solution(18371000428961818772)
XLA Ops:
  1.3 148.6 %shard_map.104 = (bf16[64,3584]{1,0:T(8,128)(2,1)}, bf16[2,128,512]{2,1,0:T(8,128)(2,1)}) custom-call(bf16[64,3584]{1,0:T(8,128)(2,1)} %tok_ref.1, f32[8,64]{1,0:T(8,128)} %bitcast.17, s32[8,64]{1,0:T(8,128)} %bitcast.18, bf16[2,3584,512]{2,1,0:T(8,128)(2,1)} %bitcast.12, bf16[512,3584]{1,0:T(8,128)(2,1)} %bitcast.13, bf16[576,512]{1,0:T(8,128)(2,1)} %bitcast.14, ...), custom_call_target="tpu_custom_call" | custom-call | tf_op jit(solution)/shard_map/pallas_call | solution.py:388
  149.9 1.8 %copy.14 = bf16[64,3584]{1,0:T(8,128)(2,1)} copy(bf16[64,3584]{1,0:T(8,128)(2,1)} %get-tuple-element.8) | data formatting | bytes 917504
  151.8 1.7 %copy.15 = bf16[1,2,128,512]{3,2,1,0:T(8,128)(2,1)} copy(bf16[1,2,128,512]{3,2,1,0:T(8,128)(2,1)} %bitcast.16) | data formatting | bytes 524288

commit v3 on v2

--- a/solution.py
+++ b/solution.py
@@ -339,19 +339,19 @@
         on_far.wait_recv()
         on_last.start()
 
+    forward(1)
     compute(0)
-    forward(1)
 
     @pl.when(outside)
     def _():
         on_last.wait_recv()
 
     spread(3)
+    forward(2)
     compute(1)
-    forward(2)
+    forward(3)
     compute(2)
     step1(2)
-    forward(3)
     step1(1)
     step2(2)
     compute(3)

time: 154 us -> 148 us (0.961)
  Pallas kernels: 149 us -> 143 us
    pallas_call x1, Pallas kernels: 149 us -> 143 us  [local_kernel(): pl.pallas_call(layer_kernel, out_shape=(jax.ShapeDtypeStruct((rows, width...]
where the time goes in v3:
time: 148 us; the launch traced here: 147 us
  Pallas kernels  143 us (97%)
  local copies, waits for them, and re-layouts  3.48 us (2%)
    pallas_call x1, Pallas kernels, local_kernel(): pl.pallas_call(layer_kernel, out_shape=(jax.ShapeDtypeStruct((rows, width...  143 us
    unnamed x2, local copies, waits for them, and re-layouts  3.48 us

profile of v3, /device:TPU:0, one launch (start us, length us, event | category | flops | bytes accessed | tf_op | source)
XLA Modules:
  0.0 147.4 jit_solution(245933242432457395)
XLA Ops:
  1.3 142.6 %shard_map.104 = (bf16[64,3584]{1,0:T(8,128)(2,1)}, bf16[2,128,512]{2,1,0:T(8,128)(2,1)}) custom-call(bf16[64,3584]{1,0:T(8,128)(2,1)} %tok_ref.1, f32[8,64]{1,0:T(8,128)} %bitcast.17, s32[8,64]{1,0:T(8,128)} %bitcast.18, bf16[2,3584,512]{2,1,0:T(8,128)(2,1)} %bitcast.12, bf16[512,3584]{1,0:T(8,128)(2,1)} %bitcast.13, bf16[576,512]{1,0:T(8,128)(2,1)} %bitcast.14, ...), custom_call_target="tpu_custom_call" | custom-call | tf_op jit(solution)/shard_map/pallas_call | solution.py:388
  143.9 1.8 %copy.14 = bf16[64,3584]{1,0:T(8,128)(2,1)} copy(bf16[64,3584]{1,0:T(8,128)(2,1)} %get-tuple-element.8) | data formatting | bytes 917504
  145.7 1.7 %copy.15 = bf16[1,2,128,512]{3,2,1,0:T(8,128)(2,1)} copy(bf16[1,2,128,512]{3,2,1,0:T(8,128)(2,1)} %bitcast.16) | data formatting | bytes 524288
